TPU v7x, 32 devices: a whole 2x2x4 slice. The times are simulated.
32 devices in a mesh: dom: 2 (over y), ffn: 4 (over z), attn: 4 (over x, core).
Axes of the slice: x: 2, y: 2, z: 4, core: 2. Of those that a mesh axis runs over, the one named last changes fastest.
Arguments:
- queries: bfloat16 [1024, 2048], P(('dom', 'ffn'), 'attn'), parts along dimension 0, may hold values from -6 to 6
- keys: bfloat16 [1024, 2048], P(('dom', 'ffn'), 'attn'), parts along dimension 0, may hold values from -6 to 6
- values: bfloat16 [1024, 2048], P(('dom', 'ffn'), 'attn'), parts along dimension 0, may hold values from -6 to 6
- residual_in: bfloat16 [1024, 2048], P(('dom', 'ffn'), 'attn'), parts along dimension 0, may hold values from -8 to 8
- flow_lengths: int32 [8, 8], P(('dom', 'ffn')), parts along dimension 0, may hold values from 0 to 16, as said below
- out_weight: bfloat16 [2048, 2048], P('attn'), may hold values from -0.125 to 0.125
- gate_weight: bfloat16 [2048, 8192], P(None, 'ffn'), may hold values from -0.125 to 0.125
- up_weight: bfloat16 [2048, 8192], P(None, 'ffn'), may hold values from -0.125 to 0.125
- down_weight: bfloat16 [8192, 2048], P('ffn'), may hold values from -0.0625 to 0.0625
Outputs:
- encoded: bfloat16 [1024, 2048], P(('dom', 'ffn', 'attn')), parts along dimension 0
There are 2 independent parts, one for each index of `dom`. A program takes and returns all parts, laid end to end along the dimension named above; an argument that names none is the same for every part. Nothing has to cross between parts.
Inputs may be any that keep to these rules, and one draw needn't show every extreme that they name: `flow_lengths`: in every group the lengths sum to at most 64, and in some group to exactly 64. The first flow of every group has exactly 16 tokens; a later flow may be empty.
All inputs are finite; a program needn't handle non-finite values.
Results may differ from a plain program's by a relative error of at most 0.015.
Values may be sent and summed in bfloat16 or wider, within the bound.
A program may use at most 128 MiB of HBM per device.

v0:
```python
import jax
import jax.numpy as jnp
from jax import lax
from jax.sharding import PartitionSpec as P

HEAD = 128


def attend(query_rows, key_rows, value_rows, segment):
    count = query_rows.shape[0]
    heads = query_rows.shape[1] // HEAD
    query_heads = query_rows.reshape(count, heads, HEAD)
    key_heads = key_rows.reshape(count, heads, HEAD)
    value_heads = value_rows.reshape(count, heads, HEAD)
    scores = jnp.einsum(
        "qhd,khd->hqk", query_heads, key_heads, preferred_element_type=jnp.float32
    ) * HEAD ** (-0.5)
    same = segment[:, None] == segment[None, :]
    scores = jnp.where(same[None], scores, -jnp.inf)
    top = jnp.max(scores, axis=2, keepdims=True)
    weights = jnp.exp(scores - top)
    probs = (weights / jnp.sum(weights, axis=2, keepdims=True)).astype(jnp.bfloat16)
    mixed = jnp.einsum("hqk,khd->qhd", probs, value_heads, preferred_element_type=jnp.float32)
    return mixed.reshape(count, heads * HEAD).astype(jnp.bfloat16)


def on_device(
    queries,
    keys,
    values,
    residual_in,
    flow_lengths,
    out_weight,
    gate_weight,
    up_weight,
    down_weight,
):
    group_rows = queries.shape[0]
    slice_width = queries.shape[1]
    head_parts = lax.axis_size("attn")
    owner = lax.axis_index("attn")
    ends = jnp.cumsum(flow_lengths[0])
    positions = jnp.arange(group_rows, dtype=jnp.int32)
    segment = jnp.sum((ends[None, :] <= positions[:, None]).astype(jnp.int32), axis=1)
    total_live = ends[-1]
    mixed = attend(queries, keys, values, segment)
    share = group_rows // head_parts
    column_start = owner * slice_width
    piece = mixed
    term = jnp.dot(piece, out_weight, preferred_element_type=jnp.float32)
    own_rows = residual_in.astype(jnp.float32)
    current = lax.dynamic_slice_in_dim(term, column_start, slice_width, 1)
    state = lax.psum_scatter(
        lax.dynamic_update_slice_in_dim(term, current + own_rows, column_start, 1).astype(
            jnp.bfloat16
        ),
        "attn",
        scatter_dimension=0,
        tiled=True,
    ).astype(jnp.float32)
    scale = lax.rsqrt(jnp.mean(state * state, axis=1, keepdims=True) + 1e-06)
    normed = (state * scale).astype(jnp.bfloat16)
    piece = lax.all_gather(normed, "ffn", axis=0, tiled=True)
    gate = jnp.dot(piece, gate_weight, preferred_element_type=jnp.float32)
    up_part = jnp.dot(piece, up_weight, preferred_element_type=jnp.float32)
    hidden = (jax.nn.silu(gate) * up_part).astype(jnp.bfloat16)
    piece = hidden
    feed = lax.psum_scatter(
        jnp.dot(piece, down_weight, preferred_element_type=jnp.float32).astype(jnp.bfloat16),
        "ffn",
        scatter_dimension=0,
        tiled=True,
    ).astype(jnp.float32)
    first_row = owner * share
    live = first_row + jnp.arange(share, dtype=jnp.int32) < total_live
    result = jnp.where(live[:, None], state + feed, 0.0).astype(jnp.bfloat16)
    return result


def solution(mesh):
    placed = (
        P(("dom", "ffn"), "attn"),
        P(("dom", "ffn"), "attn"),
        P(("dom", "ffn"), "attn"),
        P(("dom", "ffn"), "attn"),
        P(("dom", "ffn"), None),
        P("attn", None),
        P(None, "ffn"),
        P(None, "ffn"),
        P("ffn", None),
    )
    return jax.shard_map(
        on_device,
        mesh=mesh,
        in_specs=placed,
        out_specs=P(("dom", "ffn", "attn"), None),
        check_vma=False,
    )
```

profile of v0, /device:TPU:0, one launch (start us, length us, event | category | flops | bytes accessed | tf_op | source)
XLA Modules:
  0.0 100.9 jit_solution(6513386689265397479)
XLA Ops:
  6.5 0.0 reduce-scatter.3.cloned.1.call-start
  6.5 1.0 reduce-window.4
  7.5 0.1 convert_reduce_fusion
  7.6 0.1 broadcast_compare_fusion
  7.7 1.0 %copy.19 = bf16[128,512]{0,1:T(8,128)(2,1)S(1)} copy(bf16[128,512]{1,0:T(8,128)(2,1)} %param.11) | data formatting | bytes 262144 | tf_op jit(solution)/shard_map/reshape | solution.py:14
  8.7 1.2 %fusion.3 = f32[4,128,128]{1,2,0:T(8,128)S(1)} fusion(pred[128,128]{0,1:T(8,128)(4,1)S(1)} %broadcast_compare_fusion, bf16[128,512]{1,0:T(8,128)(2,1)} %param.10, bf16[128,512]{1,0:T(8,128)(2,1)} %param.9), kind=kOutput, calls=%fused_computation.6 | convolution fusion | flops 16908288 | bytes 540672 | tf_op jit(solution)/shard_map/qhd,khd->hqk/dot_general | solution.py:15
  9.9 0.1 fusion.17
  10.0 0.2 convolution_convert_fusion.1
  10.2 0.5 fusion.18
  10.7 1.0 add_dynamic-update-slice_fusion
  11.7 0.9 convert_element_type.45
  12.5 0.0 reduce-scatter.3.cloned.1.call-update
  12.5 0.0 reduce-scatter.5.cloned.1.call-start
  12.6 24.5 %reduce-scatter.3.cloned.1.call-done = bf16[32,2048]{1,0:T(8,128)(2,1)} async-done(((bf16[128,2048]{1,0:T(8,128)(2,1)}), bf16[32,2048]{1,0:T(8,128)(2,1)}) %reduce-scatter.3.cloned.1.call-update) | async-done | bytes 131088 | tf_op jit(solution)/shard_map/reduce_scatter | solution.py:53
  37.1 1.0 %fusion.6 = f32[32]{0:T(128)S(1)} fusion(bf16[32,2048]{1,0:T(8,128)(2,1)} %reduce-scatter.3.cloned.1.call-done), kind=kLoop, calls=%fused_computation.13 | loop fusion | flops 196576 | bytes 131200 | tf_op jit(solution)/shard_map/reduce_sum | solution.py:61
  38.1 1.0 fusion.7
  39.1 15.6 %all_gather.3 = bf16[128,2048]{1,0:T(8,128)(2,1)S(1)} all-gather(bf16[32,2048]{1,0:T(8,128)(2,1)S(1)} %fusion.7), channel_id=1, replica_groups=mesh['dom'=2,'ffn'=4,'attn'=4] {'ffn'}, dimensions={0}, use_global_device_ids=true | all-gather | bytes 655360 | tf_op jit(solution)/shard_map/all_gather | solution.py:63
  54.7 5.6 %fusion.19 = f32[128,2048]{1,0:T(8,128)} fusion(bf16[128,2048]{1,0:T(8,128)(2,1)S(1)} %all_gather.3, bf16[2048,2048]{1,0:T(8,128)(2,1)} %param.15), kind=kOutput, calls=%fused_computation.33 | convolution fusion | flops 1073741824 | bytes 9961472 | tf_op jit(solution)/shard_map/dot_general | solution.py:64
  60.4 9.5 %convolution_convert_fusion = bf16[128,2048]{1,0:T(8,128)(2,1)} fusion(bf16[2048,2048]{1,0:T(8,128)(2,1)} %param.17, bf16[128,2048]{1,0:T(8,128)(2,1)S(1)} %all_gather.3, bf16[2048,2048]{1,0:T(8,128)(2,1)} %param.16, f32[128,2048]{1,0:T(8,128)} %fusion.19), kind=kOutput, calls=%fused_computation.2 | convolution fusion | flops 2149318656 | bytes 18874368 | tf_op jit(solution)/shard_map/dot_general | solution.py:69
  69.8 0.0 reduce-scatter.5.cloned.1.call-update
  69.9 0.6 slice.4
  70.4 0.7 add_compare_fusion
  71.1 21.3 %reduce-scatter.5.cloned.1.call-done = bf16[32,2048]{1,0:T(8,128)(2,1)} async-done(((bf16[128,2048]{1,0:T(8,128)(2,1)}), bf16[32,2048]{1,0:T(8,128)(2,1)}) %reduce-scatter.5.cloned.1.call-update) | async-done | bytes 131088 | tf_op jit(solution)/shard_map/reduce_scatter | solution.py:68
  92.4 1.6 %fusion.9 = bf16[32,2048]{1,0:T(8,128)(2,1)} fusion(bf16[32,2048]{1,0:T(8,128)(2,1)S(1)} %copy-done.1, bf16[32,2048]{1,0:T(8,128)(2,1)} %reduce-scatter.5.cloned.1.call-done, pred[32]{0:T(512)(128)(4,1)S(1)} %add_compare_fusion), kind=kLoop, calls=%fused_computation.16 | loop fusion | flops 327680 | bytes 393248 | tf_op jit(solution)/shard_map/convert_element_type | solution.py:76
  (5 shorter events, 0.0 us)
Async XLA Ops:
  6.5 3.7 %copy-start = (bf16[512,2048]{1,0:T(8,128)(2,1)S(1)}, bf16[512,2048]{1,0:T(8,128)(2,1)}, u32[]{:S(2)}) copy-start(bf16[512,2048]{1,0:T(8,128)(2,1)} %param.14) | copy-start | bytes 6291460
  6.5 30.5 %reduce-scatter.3.cloned.1.call-start = ((), (), s32[]{:S(2)}) async-start(), calls=%async_computation.2 | async-start | bytes 655360 | tf_op jit(solution)/shard_map/reduce_scatter | solution.py:53
  12.5 79.9 %reduce-scatter.5.cloned.1.call-start = ((), (), s32[]{:S(2)}) async-start(), calls=%async_computation.3 | async-start | bytes 655360 | tf_op jit(solution)/shard_map/reduce_scatter | solution.py:68
  60.4 32.1 %copy-start.1 = (bf16[32,2048]{1,0:T(8,128)(2,1)S(1)}, bf16[32,2048]{1,0:T(8,128)(2,1)}, u32[]{:S(2)}) copy-start(bf16[32,2048]{1,0:T(8,128)(2,1)} %reduce-scatter.3.cloned.1.call-done) | copy-start | bytes 393220
Sparse Core Ops, SparseCore 0:
  12.7 24.3 reduce-scatter.2
  70.0 22.4 reduce-scatter.4
where the time goes:
time: 101 us
  waiting for transfers between devices  45.8 us (45%)
  matrix products  17 us (17%)
  blocking collectives  15.6 us (15%)
  between operations  13.5 us (13%)
  other arithmetic  7.38 us (7%)
  local copies, waits for them, and re-layouts  1.61 us (2%)
    reduce_scatter x1, waiting for transfers between devices, on_device(): lax.psum_scatter(lax.dynamic_update_slice_in_dim(term, current + own_rows...  24.5 us
    reduce_scatter x1, waiting for transfers between devices, on_device(): lax.psum_scatter(jnp.dot(piece, down_weight, preferred_element_type=jnp.f...  21.3 us
    all_gather x1, blocking collectives, on_device(): piece = lax.all_gather(normed, 'ffn', axis=0, tiled=True)  15.6 us
    dot_general x1, matrix products, on_device(): jnp.dot(piece, down_weight, preferred_element_type=jnp.float32)  9.47 us
    dot_general x1, matrix products, on_device(): gate = jnp.dot(piece, gate_weight, preferred_element_type=jnp.float32)  5.63 us
  transfers between devices with their start and end apart: 2, of which 2 were waited for; matrix products, arithmetic and copies ran while one was open for 1% of the time, Pallas kernels for 0%

commit v1 on v0

v1 whole, which is shorter than its diff:
```python
import functools

import jax
import jax.numpy as jnp
from jax import lax
from jax.experimental import pallas as pl
from jax.experimental.pallas import tpu as pltpu
from jax.sharding import PartitionSpec as P

HEAD = 128
LIVE = 64
ROWS = 16
PARTS = LIVE // ROWS
MESH = pl.DeviceIdType.MESH
F32 = jnp.float32
BF16 = jnp.bfloat16


def widths(total, width):
    width = min(width, total)
    return [(at, width) for at in range(0, total, width)]


def layer(
    n_attn,
    n_ffn,
    q_hbm,
    k_hbm,
    v_hbm,
    res_hbm,
    lens,
    wo_hbm,
    wg_hbm,
    wu_hbm,
    wd_hbm,
    out,
    q,
    k,
    v,
    res,
    wo,
    wg,
    wu,
    wd,
    mixed,
    term,
    term16,
    got1,
    state,
    rows,
    gate,
    up,
    hidden,
    part16,
    got2,
    done16,
    in_sem,
    gate_sem,
    up_sem,
    down_sem,
    send1,
    recv1,
    send2,
    recv2,
    send3,
    recv3,
    send4,
    recv4,
):
    a = lax.axis_index("attn")
    z = lax.axis_index("ffn")
    width = q.shape[1]
    model = wo.shape[1]
    units = wg.shape[1]
    share = out.shape[0]
    part = lax.rem(a, PARTS)
    own_rows = pl.ds(pl.multiple_of(part * ROWS, ROWS), ROWS)

    barrier = pltpu.get_barrier_semaphore()
    for step in range(1, n_attn):
        pl.semaphore_signal(
            barrier, inc=1, device_id={"attn": lax.rem(a + step, n_attn)}, device_id_type=MESH
        )
    for step in range(1, n_ffn):
        pl.semaphore_signal(
            barrier, inc=1, device_id={"ffn": lax.rem(z + step, n_ffn)}, device_id_type=MESH
        )

    live_rows = pl.ds(0, LIVE)
    small = [
        pltpu.make_async_copy(src.at[live_rows, :], dst, in_sem.at[i])
        for i, (src, dst) in enumerate(((q_hbm, q), (k_hbm, k), (v_hbm, v), (res_hbm, res)))
    ]
    small.append(pltpu.make_async_copy(wo_hbm, wo, in_sem.at[4]))
    for copy in small:
        copy.start()
    deep = widths(model, 512)
    wide = widths(model, 512)
    gate_in = [
        pltpu.make_async_copy(wg_hbm.at[pl.ds(at, w), :], wg.at[pl.ds(at, w), :], gate_sem.at[i])
        for i, (at, w) in enumerate(deep)
    ]
    up_in = [
        pltpu.make_async_copy(wu_hbm.at[pl.ds(at, w), :], wu.at[pl.ds(at, w), :], up_sem.at[i])
        for i, (at, w) in enumerate(deep)
    ]
    down_in = [
        pltpu.make_async_copy(wd_hbm.at[:, pl.ds(at, w)], wd.at[:, pl.ds(at, w)], down_sem.at[i])
        for i, (at, w) in enumerate(wide)
    ]
    for copy in small[:3]:
        copy.wait()
    for one, two in zip(gate_in, up_in):
        one.start()
        two.start()
    for copy in down_in:
        copy.start()

    row_at = lax.broadcasted_iota(jnp.int32, (LIVE, LIVE), 0)
    col_at = lax.broadcasted_iota(jnp.int32, (LIVE, LIVE), 1)
    row_flow = jnp.zeros((LIVE, LIVE), jnp.int32)
    col_flow = jnp.zeros((LIVE, LIVE), jnp.int32)
    end = jnp.int32(0)
    for flow in range(lens.shape[1]):
        end = end + lens[0, flow]
        row_flow += (row_at >= end).astype(jnp.int32)
        col_flow += (col_at >= end).astype(jnp.int32)
    total_live = end
    same = row_flow == col_flow
    for head in range(width // HEAD):
        cols = slice(head * HEAD, (head + 1) * HEAD)
        scores = lax.dot_general(
            q[:, cols], k[:, cols], (((1,), (1,)), ((), ())), preferred_element_type=F32
        ) * HEAD ** (-0.5)
        scores = jnp.where(same, scores, -jnp.inf)
        weights = jnp.exp(scores - jnp.max(scores, axis=1, keepdims=True))
        probs = (weights / jnp.sum(weights, axis=1, keepdims=True)).astype(BF16)
        mixed[:, cols] = jnp.dot(probs, v[:, cols], preferred_element_type=F32).astype(BF16)

    small[3].wait()
    small[4].wait()
    pl.semaphore_wait(barrier, n_attn + n_ffn - 2)
    sent = []
    first = []
    for i, (at, w) in enumerate(wide):
        for sub in range(at, at + w, width):
            cols = slice(sub, sub + width)
            value = jnp.dot(mixed[...], wo[:, cols], preferred_element_type=F32)
            value += jnp.where(a == sub // width, res[...].astype(F32), 0.0)
            term[:, cols] = value
            term16[:, cols] = value.astype(BF16)
        for step in range(1, n_attn):
            peer = lax.rem(a + step, n_attn)
            peer_rows = pl.ds(pl.multiple_of(lax.rem(peer, PARTS) * ROWS, ROWS), ROWS)
            copy = pltpu.make_async_remote_copy(
                src_ref=term16.at[peer_rows, pl.ds(at, w)],
                dst_ref=got1.at[step - 1, :, pl.ds(at, w)],
                send_sem=send1.at[step - 1, i],
                recv_sem=recv1.at[step - 1, i],
                device_id={"attn": peer},
                device_id_type=MESH,
            )
            copy.start()
            sent.append(copy)
            first.append(copy)
    squares = jnp.zeros((ROWS, 1), F32)
    for i, (at, w) in enumerate(wide):
        cols = slice(at, at + w)
        value = term[own_rows, cols]
        for step in range(1, n_attn):
            first[i * (n_attn - 1) + step - 1].wait_recv()
            value += got1[step - 1, :, cols].astype(F32)
        state[:, cols] = value
        squares += jnp.sum(value * value, axis=1, keepdims=True)
    scale = lax.rsqrt(squares / model + 1e-06)

    second = []
    for i, (at, w) in enumerate(deep):
        rows[0:ROWS, at : at + w] = (state[:, at : at + w] * scale).astype(BF16)
        for step in range(1, n_ffn):
            copy = pltpu.make_async_remote_copy(
                src_ref=rows.at[pl.ds(0, ROWS), pl.ds(at, w)],
                dst_ref=rows.at[pl.ds(step * ROWS, ROWS), pl.ds(at, w)],
                send_sem=send2.at[step - 1, i],
                recv_sem=recv2.at[step - 1, i],
                device_id={"ffn": lax.rem(z + step, n_ffn)},
                device_id_type=MESH,
            )
            copy.start()
            sent.append(copy)
            second.append(copy)

    for i, (at, w) in enumerate(deep):
        gate_in[i].wait()
        up_in[i].wait()
        for step in range(1, n_ffn):
            second[i * (n_ffn - 1) + step - 1].wait_recv()
        for col, cw in widths(units, 512):
            cols = slice(col, col + cw)
            piece = rows[:, at : at + w]
            g = jnp.dot(piece, wg[at : at + w, cols], preferred_element_type=F32)
            u = jnp.dot(piece, wu[at : at + w, cols], preferred_element_type=F32)
            if i > 0:
                g += gate[:, cols]
                u += up[:, cols]
            if i < len(deep) - 1:
                gate[:, cols] = g
                up[:, cols] = u
            else:
                hidden[:, cols] = (g / (1.0 + jnp.exp(-g)) * u).astype(BF16)

    third = []
    for i, (at, w) in enumerate(wide):
        cols = slice(at, at + w)
        down_in[i].wait()
        part16[:, cols] = jnp.dot(hidden[...], wd[:, cols], preferred_element_type=F32).astype(BF16)
        for step in range(1, n_ffn):
            copy = pltpu.make_async_remote_copy(
                src_ref=part16.at[pl.ds(step * ROWS, ROWS), pl.ds(at, w)],
                dst_ref=got2.at[step - 1, :, pl.ds(at, w)],
                send_sem=send3.at[step - 1, i],
                recv_sem=recv3.at[step - 1, i],
                device_id={"ffn": lax.rem(z + n_ffn - step, n_ffn)},
                device_id_type=MESH,
            )
            copy.start()
            sent.append(copy)
            third.append(copy)

    @pl.when(a * share >= LIVE)
    def _():
        out[...] = jnp.zeros_like(out)

    live = part * ROWS + lax.broadcasted_iota(jnp.int32, (ROWS, 1), 0) < total_live

    def last(p, i, at, w):
        return pltpu.make_async_remote_copy(
            src_ref=done16.at[:, pl.ds(at, w)],
            dst_ref=out.at[pl.ds(p * ROWS % share, ROWS), pl.ds(at, w)],
            send_sem=send4.at[i],
            recv_sem=recv4.at[p, i],
            device_id={"attn": p * ROWS // share},
            device_id_type=MESH,
        )

    for i, (at, w) in enumerate(wide):
        cols = slice(at, at + w)
        feed = part16[0:ROWS, cols].astype(F32)
        for step in range(1, n_ffn):
            third[i * (n_ffn - 1) + step - 1].wait_recv()
            feed += got2[step - 1, :, cols].astype(F32)
        done16[:, cols] = jnp.where(live, state[:, cols] + feed, 0.0).astype(BF16)
        for p in range(PARTS):
            owner = p * ROWS // share

            @pl.when(a == p)
            def _():
                if owner == p:
                    out[p * ROWS % share : p * ROWS % share + ROWS, cols] = done16[:, cols]
                else:
                    last(p, i, at, w).start()

    for copy in sent:
        copy.wait_send()
    for p in range(PARTS):
        owner = p * ROWS // share
        if owner != p:

            @pl.when(a == p)
            def _():
                for i, (at, w) in enumerate(wide):
                    last(p, i, at, w).wait_send()

            @pl.when(a == owner)
            def _():
                for i, (at, w) in enumerate(wide):
                    last(p, i, at, w).wait_recv()


def on_device(n_attn, n_ffn, q, k, v, res, lens, wo, wg, wu, wd):
    group, width = q.shape
    model = wo.shape[1]
    units = wg.shape[1]
    share = group // n_attn
    tokens = n_ffn * ROWS
    pieces = max(1, model // 512)
    any_space = pl.BlockSpec(memory_space=pl.ANY)
    dma = pltpu.SemaphoreType.DMA
    return pl.pallas_call(
        functools.partial(layer, n_attn, n_ffn),
        out_shape=jax.ShapeDtypeStruct((share, model), BF16),
        in_specs=[any_space] * 4 + [pl.BlockSpec(memory_space=pltpu.SMEM)] + [any_space] * 4,
        out_specs=pl.BlockSpec(memory_space=pltpu.VMEM),
        scratch_shapes=[
            pltpu.VMEM((LIVE, width), BF16),
            pltpu.VMEM((LIVE, width), BF16),
            pltpu.VMEM((LIVE, width), BF16),
            pltpu.VMEM((LIVE, width), BF16),
            pltpu.VMEM((width, model), BF16),
            pltpu.VMEM((model, units), BF16),
            pltpu.VMEM((model, units), BF16),
            pltpu.VMEM((units, model), BF16),
            pltpu.VMEM((LIVE, width), BF16),
            pltpu.VMEM((LIVE, model), F32),
            pltpu.VMEM((LIVE, model), BF16),
            pltpu.VMEM((n_attn - 1, ROWS, model), BF16),
            pltpu.VMEM((ROWS, model), F32),
            pltpu.VMEM((tokens, model), BF16),
            pltpu.VMEM((tokens, units), F32),
            pltpu.VMEM((tokens, units), F32),
            pltpu.VMEM((tokens, units), BF16),
            pltpu.VMEM((tokens, model), BF16),
            pltpu.VMEM((n_ffn - 1, ROWS, model), BF16),
            pltpu.VMEM((ROWS, model), BF16),
            dma((5,)),
            dma((pieces,)),
            dma((pieces,)),
            dma((pieces,)),
            dma((n_attn - 1, pieces)),
            dma((n_attn - 1, pieces)),
            dma((n_ffn - 1, pieces)),
            dma((n_ffn - 1, pieces)),
            dma((n_ffn - 1, pieces)),
            dma((n_ffn - 1, pieces)),
            dma((pieces,)),
            dma((PARTS, pieces)),
        ],
        compiler_params=pltpu.CompilerParams(
            collective_id=0, has_side_effects=True, vmem_limit_bytes=56 * 1024 * 1024
        ),
        cost_estimate=pl.CostEstimate(
            flops=2 * tokens * 3 * model * units + 2 * LIVE * width * model,
            bytes_accessed=2 * (3 * model * units + width * model),
            transcendentals=tokens * units,
        ),
    )(q, k, v, res, lens, wo, wg, wu, wd)


def solution(mesh):
    rows_split = P(("dom", "ffn"), "attn")
    placed = (
        rows_split,
        rows_split,
        rows_split,
        rows_split,
        P(("dom", "ffn"), None),
        P("attn", None),
        P(None, "ffn"),
        P(None, "ffn"),
        P("ffn", None),
    )
    return jax.shard_map(
        functools.partial(on_device, mesh.shape["attn"], mesh.shape["ffn"]),
        mesh=mesh,
        in_specs=placed,
        out_specs=P(("dom", "ffn", "attn"), None),
        check_vma=False,
    )
```

time: 101 us -> 31.5 us (0.31)
  the two profiles are of different devices: /device:TPU:0 before, /device:TPU:1 now
where the time goes in v1:
time: 31.5 us; the launch traced here: 31.4 us
  Pallas kernels  29.8 us (95%)
  local copies, waits for them, and re-layouts  1.57 us (5%)
    pallas_call x1, Pallas kernels, on_device(): pl.pallas_call(functools.partial(layer, n_attn, n_ffn), out_shape=jax.Sha...  29.8 us
    unnamed x1, local copies, waits for them, and re-layouts  1.57 us

profile of v1, /device:TPU:1, one launch (start us, length us, event | category | flops | bytes accessed | tf_op | source)
XLA Modules:
  0.0 31.4 jit_solution(1254799926511256654)
XLA Ops:
  0.0 29.8 %shard_map.91 = bf16[32,2048]{1,0:T(8,128)(2,1)} custom-call(bf16[128,512]{1,0:T(8,128)(2,1)} %q_hbm.1, bf16[128,512]{1,0:T(8,128)(2,1)} %k_hbm.1, bf16[128,512]{1,0:T(8,128)(2,1)} %v_hbm.1, bf16[128,512]{1,0:T(8,128)(2,1)} %res_hbm.1, s32[1,8]{1,0:T(1,128)} %lens.1, bf16[512,2048]{1,0:T(8,128)(2,1)} %wo_hbm.1, bf16[2048,2048]{1,0:T(8,128)(2,1)} %wg_hbm.1, ...), custom_call_target="tpu_custom_call" | custom-call | flops 1744830464 | bytes 27262976 | tf_op jit(solution)/shard_map/pallas_call | solution.py:289
  29.8 1.6 %copy.11 = bf16[32,2048]{1,0:T(8,128)(2,1)} copy(bf16[32,2048]{1,0:T(8,128)(2,1)} %shard_map.91) | data formatting | bytes 262144

commit v2 on v1

--- a/solution.py
+++ b/solution.py
@@ -53,7 +53,7 @@
     hidden,
     part16,
     got2,
-    done16,
+    held,
     in_sem,
     gate_sem,
     up_sem,
@@ -74,17 +74,17 @@
     units = wg.shape[1]
     share = out.shape[0]
     part = lax.rem(a, PARTS)
+    owner = part * ROWS // share
+    place = lax.rem(part * ROWS, share) // ROWS
+    away = jnp.logical_and(a < PARTS, a != owner)
     own_rows = pl.ds(pl.multiple_of(part * ROWS, ROWS), ROWS)
 
     barrier = pltpu.get_barrier_semaphore()
-    for step in range(1, n_attn):
-        pl.semaphore_signal(
-            barrier, inc=1, device_id={"attn": lax.rem(a + step, n_attn)}, device_id_type=MESH
-        )
-    for step in range(1, n_ffn):
-        pl.semaphore_signal(
-            barrier, inc=1, device_id={"ffn": lax.rem(z + step, n_ffn)}, device_id_type=MESH
-        )
+    for far in range(n_ffn):
+        for step in range(n_attn):
+            if far or step:
+                peer = {"ffn": lax.rem(z + far, n_ffn), "attn": lax.rem(a + step, n_attn)}
+                pl.semaphore_signal(barrier, inc=1, device_id=peer, device_id_type=MESH)
 
     live_rows = pl.ds(0, LIVE)
     small = [
@@ -139,7 +139,7 @@
 
     small[3].wait()
     small[4].wait()
-    pl.semaphore_wait(barrier, n_attn + n_ffn - 2)
+    pl.semaphore_wait(barrier, n_attn * n_ffn - 1)
     sent = []
     first = []
     for i, (at, w) in enumerate(wide):
@@ -163,20 +163,16 @@
             copy.start()
             sent.append(copy)
             first.append(copy)
-    squares = jnp.zeros((ROWS, 1), F32)
-    for i, (at, w) in enumerate(wide):
+
+    second = []
+    for i, (at, w) in enumerate(deep):
         cols = slice(at, at + w)
         value = term[own_rows, cols]
         for step in range(1, n_attn):
             first[i * (n_attn - 1) + step - 1].wait_recv()
             value += got1[step - 1, :, cols].astype(F32)
         state[:, cols] = value
-        squares += jnp.sum(value * value, axis=1, keepdims=True)
-    scale = lax.rsqrt(squares / model + 1e-06)
-
-    second = []
-    for i, (at, w) in enumerate(deep):
-        rows[0:ROWS, at : at + w] = (state[:, at : at + w] * scale).astype(BF16)
+        rows[0:ROWS, cols] = value.astype(BF16)
         for step in range(1, n_ffn):
             copy = pltpu.make_async_remote_copy(
                 src_ref=rows.at[pl.ds(0, ROWS), pl.ds(at, w)],
@@ -189,15 +185,34 @@
             copy.start()
             sent.append(copy)
             second.append(copy)
-
+    state_copy = pltpu.make_async_remote_copy(
+        src_ref=state,
+        dst_ref=held.at[place],
+        send_sem=send4.at[0],
+        recv_sem=recv4.at[place],
+        device_id={"attn": owner},
+        device_id_type=MESH,
+    )
+
+    @pl.when(away)
+    def _():
+        state_copy.start()
+
+    @pl.when(a == owner)
+    def _():
+        held[place] = state[...]
+
+    squares = jnp.zeros((n_ffn * ROWS, 1), F32)
     for i, (at, w) in enumerate(deep):
         gate_in[i].wait()
         up_in[i].wait()
         for step in range(1, n_ffn):
             second[i * (n_ffn - 1) + step - 1].wait_recv()
+        piece = rows[:, at : at + w]
+        squares += jnp.sum(piece.astype(F32) * piece.astype(F32), axis=1, keepdims=True)
+        scale = lax.rsqrt(squares / model + 1e-06)
         for col, cw in widths(units, 512):
             cols = slice(col, col + cw)
-            piece = rows[:, at : at + w]
             g = jnp.dot(piece, wg[at : at + w, cols], preferred_element_type=F32)
             u = jnp.dot(piece, wu[at : at + w, cols], preferred_element_type=F32)
             if i > 0:
@@ -207,74 +222,101 @@
                 gate[:, cols] = g
                 up[:, cols] = u
             else:
+                g *= scale
+                u *= scale
                 hidden[:, cols] = (g / (1.0 + jnp.exp(-g)) * u).astype(BF16)
 
-    third = []
+    def partial(step, i, at, w):
+        return pltpu.make_async_remote_copy(
+            src_ref=part16.at[pl.ds(step * ROWS, ROWS), pl.ds(at, w)],
+            dst_ref=got2.at[place, step, :, pl.ds(at, w)],
+            send_sem=send3.at[step, i],
+            recv_sem=recv3.at[place, step, i],
+            device_id={"ffn": lax.rem(z + n_ffn - step, n_ffn), "attn": owner},
+            device_id_type=MESH,
+        )
+
     for i, (at, w) in enumerate(wide):
         cols = slice(at, at + w)
         down_in[i].wait()
         part16[:, cols] = jnp.dot(hidden[...], wd[:, cols], preferred_element_type=F32).astype(BF16)
-        for step in range(1, n_ffn):
-            copy = pltpu.make_async_remote_copy(
+
+        @pl.when(a < PARTS)
+        def _():
+            for step in range(1, n_ffn):
+                partial(step, i, at, w).start()
+
+        @pl.when(away)
+        def _():
+            partial(0, i, at, w).start()
+
+        @pl.when(a == owner)
+        def _():
+            got2[place, 0, :, cols] = part16[0:ROWS, cols]
+
+    per = share // ROWS
+
+    @pl.when(a * share >= LIVE)
+    def _():
+        out[...] = jnp.zeros_like(out)
+
+    @pl.when(a * share < LIVE)
+    def _():
+        def arrival(q, step, i, at, w):
+            return pltpu.make_async_remote_copy(
                 src_ref=part16.at[pl.ds(step * ROWS, ROWS), pl.ds(at, w)],
-                dst_ref=got2.at[step - 1, :, pl.ds(at, w)],
-                send_sem=send3.at[step - 1, i],
-                recv_sem=recv3.at[step - 1, i],
-                device_id={"ffn": lax.rem(z + n_ffn - step, n_ffn)},
+                dst_ref=got2.at[q, step, :, pl.ds(at, w)],
+                send_sem=send3.at[step, i],
+                recv_sem=recv3.at[q, step, i],
+                device_id={"attn": owner},
                 device_id_type=MESH,
             )
-            copy.start()
-            sent.append(copy)
-            third.append(copy)
-
-    @pl.when(a * share >= LIVE)
-    def _():
-        out[...] = jnp.zeros_like(out)
-
-    live = part * ROWS + lax.broadcasted_iota(jnp.int32, (ROWS, 1), 0) < total_live
-
-    def last(p, i, at, w):
-        return pltpu.make_async_remote_copy(
-            src_ref=done16.at[:, pl.ds(at, w)],
-            dst_ref=out.at[pl.ds(p * ROWS % share, ROWS), pl.ds(at, w)],
-            send_sem=send4.at[i],
-            recv_sem=recv4.at[p, i],
-            device_id={"attn": p * ROWS // share},
-            device_id_type=MESH,
-        )
-
-    for i, (at, w) in enumerate(wide):
-        cols = slice(at, at + w)
-        feed = part16[0:ROWS, cols].astype(F32)
-        for step in range(1, n_ffn):
-            third[i * (n_ffn - 1) + step - 1].wait_recv()
-            feed += got2[step - 1, :, cols].astype(F32)
-        done16[:, cols] = jnp.where(live, state[:, cols] + feed, 0.0).astype(BF16)
-        for p in range(PARTS):
-            owner = p * ROWS // share
-
-            @pl.when(a == p)
+
+        for q in range(per):
+
+            @pl.when(a * per + q != a)
             def _():
-                if owner == p:
-                    out[p * ROWS % share : p * ROWS % share + ROWS, cols] = done16[:, cols]
-                else:
-                    last(p, i, at, w).start()
+                pltpu.make_async_remote_copy(
+                    src_ref=state,
+                    dst_ref=held.at[q],
+                    send_sem=send4.at[0],
+                    recv_sem=recv4.at[q],
+                    device_id={"attn": owner},
+                    device_id_type=MESH,
+                ).wait_recv()
+
+        at_row = lax.broadcasted_iota(jnp.int32, (ROWS, 1), 0)
+        for i, (at, w) in enumerate(wide):
+            cols = slice(at, at + w)
+            for q in range(per):
+
+                @pl.when(a * per + q != a)
+                def _():
+                    arrival(q, 0, i, at, w).wait_recv()
+
+                for step in range(1, n_ffn):
+                    arrival(q, step, i, at, w).wait_recv()
+                feed = got2[q, 0, :, cols].astype(F32)
+                for step in range(1, n_ffn):
+                    feed += got2[q, step, :, cols].astype(F32)
+                live = (a * per + q) * ROWS + at_row < total_live
+                value = jnp.where(live, held[q, :, cols] + feed, 0.0)
+                out[q * ROWS : (q + 1) * ROWS, cols] = value.astype(BF16)
 
     for copy in sent:
         copy.wait_send()
-    for p in range(PARTS):
-        owner = p * ROWS // share
-        if owner != p:
-
-            @pl.when(a == p)
-            def _():
-                for i, (at, w) in enumerate(wide):
-                    last(p, i, at, w).wait_send()
-
-            @pl.when(a == owner)
-            def _():
-                for i, (at, w) in enumerate(wide):
-                    last(p, i, at, w).wait_recv()
+
+    @pl.when(a < PARTS)
+    def _():
+        for i, (at, w) in enumerate(wide):
+            for step in range(1, n_ffn):
+                partial(step, i, at, w).wait_send()
+
+    @pl.when(away)
+    def _():
+        state_copy.wait_send()
+        for i, (at, w) in enumerate(wide):
+            partial(0, i, at, w).wait_send()
 
 
 def on_device(n_attn, n_ffn, q, k, v, res, lens, wo, wg, wu, wd):
@@ -283,12 +325,13 @@
     units = wg.shape[1]
     share = group // n_attn
     tokens = n_ffn * ROWS
+    per = share // ROWS
     pieces = max(1, model // 512)
     any_space = pl.BlockSpec(memory_space=pl.ANY)
     dma = pltpu.SemaphoreType.DMA
     return pl.pallas_call(
         functools.partial(layer, n_attn, n_ffn),
-        out_shape=jax.ShapeDtypeStruct((share, model), BF16),
+        out_shape=pltpu.VMEM((share, model), BF16),
         in_specs=[any_space] * 4 + [pl.BlockSpec(memory_space=pltpu.SMEM)] + [any_space] * 4,
         out_specs=pl.BlockSpec(memory_space=pltpu.VMEM),
         scratch_shapes=[
@@ -310,8 +353,8 @@
             pltpu.VMEM((tokens, units), F32),
             pltpu.VMEM((tokens, units), BF16),
             pltpu.VMEM((tokens, model), BF16),
-            pltpu.VMEM((n_ffn - 1, ROWS, model), BF16),
-            pltpu.VMEM((ROWS, model), BF16),
+            pltpu.VMEM((per, n_ffn, ROWS, model), BF16),
+            pltpu.VMEM((per, ROWS, model), F32),
             dma((5,)),
             dma((pieces,)),
             dma((pieces,)),
@@ -320,10 +363,10 @@
             dma((n_attn - 1, pieces)),
             dma((n_ffn - 1, pieces)),
             dma((n_ffn - 1, pieces)),
-            dma((n_ffn - 1, pieces)),
-            dma((n_ffn - 1, pieces)),
-            dma((pieces,)),
-            dma((PARTS, pieces)),
+            dma((n_ffn, pieces)),
+            dma((per, n_ffn, pieces)),
+            dma((1,)),
+            dma((per,)),
         ],
         compiler_params=pltpu.CompilerParams(
             collective_id=0, has_side_effects=True, vmem_limit_bytes=56 * 1024 * 1024

time: 31.5 us -> 27.8 us (0.88)
  Pallas kernels: 29.8 us -> 27 us
  local copies, waits for them, and re-layouts: 1.57 us -> 0.66 us
    pallas_call x1, Pallas kernels: 29.8 us -> 27 us  [on_device(): pl.pallas_call(functools.partial(layer, n_attn, n_ffn), out_shape=pltpu.V...]
    unnamed x1, local copies, waits for them, and re-layouts: 1.57 us -> 0.66 us
where the time goes in v2:
time: 27.8 us; the launch traced here: 27.6 us
  Pallas kernels  27 us (97%)
  local copies, waits for them, and re-layouts  0.66 us (2%)
    pallas_call x1, Pallas kernels, on_device(): pl.pallas_call(functools.partial(layer, n_attn, n_ffn), out_shape=pltpu.V...  27 us
    unnamed x1, local copies, waits for them, and re-layouts  0.66 us

profile of v2, /device:TPU:1, one launch (start us, length us, event | category | flops | bytes accessed | tf_op | source)
XLA Modules:
  0.0 27.6 jit_solution(1281274710263137376)
XLA Ops:
  0.0 27.0 %shard_map.91 = bf16[32,2048]{1,0:T(8,128)(2,1)S(1)} custom-call(bf16[128,512]{1,0:T(8,128)(2,1)} %q_hbm.1, bf16[128,512]{1,0:T(8,128)(2,1)} %k_hbm.1, bf16[128,512]{1,0:T(8,128)(2,1)} %v_hbm.1, bf16[128,512]{1,0:T(8,128)(2,1)} %res_hbm.1, s32[1,8]{1,0:T(1,128)} %lens.1, bf16[512,2048]{1,0:T(8,128)(2,1)} %wo_hbm.1, bf16[2048,2048]{1,0:T(8,128)(2,1)} %wg_hbm.1, ...), custom_call_target="tpu_custom_call" | custom-call | flops 1744830464 | bytes 27262976 | tf_op jit(solution)/shard_map/pallas_call | solution.py:332
  27.0 0.7 %copy.11 = bf16[32,2048]{1,0:T(8,128)(2,1)} copy(bf16[32,2048]{1,0:T(8,128)(2,1)S(1)} %shard_map.91) | data formatting | bytes 262144

commit v3 on v2

--- a/solution.py
+++ b/solution.py
@@ -127,21 +127,30 @@
         col_flow += (col_at >= end).astype(jnp.int32)
     total_live = end
     same = row_flow == col_flow
-    for head in range(width // HEAD):
-        cols = slice(head * HEAD, (head + 1) * HEAD)
-        scores = lax.dot_general(
+    heads = [slice(at, at + HEAD) for at in range(0, width, HEAD)]
+    scores = [
+        lax.dot_general(
             q[:, cols], k[:, cols], (((1,), (1,)), ((), ())), preferred_element_type=F32
-        ) * HEAD ** (-0.5)
-        scores = jnp.where(same, scores, -jnp.inf)
-        weights = jnp.exp(scores - jnp.max(scores, axis=1, keepdims=True))
-        probs = (weights / jnp.sum(weights, axis=1, keepdims=True)).astype(BF16)
-        mixed[:, cols] = jnp.dot(probs, v[:, cols], preferred_element_type=F32).astype(BF16)
+        )
+        for cols in heads
+    ]
+    scores = [jnp.where(same, score * HEAD ** (-0.5), -jnp.inf) for score in scores]
+    tops = [jnp.max(score, axis=1, keepdims=True) for score in scores]
+    weights = [jnp.exp(score - top) for score, top in zip(scores, tops)]
+    sums = [jnp.sum(weight, axis=1, keepdims=True) for weight in weights]
+    probs = [(weight / total).astype(BF16) for weight, total in zip(weights, sums)]
+    outs = [
+        jnp.dot(prob, v[:, cols], preferred_element_type=F32).astype(BF16)
+        for prob, cols in zip(probs, heads)
+    ]
+    for cols, value in zip(heads, outs):
+        mixed[:, cols] = value
 
     small[3].wait()
     small[4].wait()
     pl.semaphore_wait(barrier, n_attn * n_ffn - 1)
     sent = []
-    first = []
+    first = {}
     for i, (at, w) in enumerate(wide):
         for sub in range(at, at + w, width):
             cols = slice(sub, sub + width)
@@ -149,7 +158,7 @@
             value += jnp.where(a == sub // width, res[...].astype(F32), 0.0)
             term[:, cols] = value
             term16[:, cols] = value.astype(BF16)
-        for step in range(1, n_attn):
+        for step in sorted(range(1, n_attn), key=lambda far: -min(far, n_attn - far)):
             peer = lax.rem(a + step, n_attn)
             peer_rows = pl.ds(pl.multiple_of(lax.rem(peer, PARTS) * ROWS, ROWS), ROWS)
             copy = pltpu.make_async_remote_copy(
@@ -162,14 +171,14 @@
             )
             copy.start()
             sent.append(copy)
-            first.append(copy)
+            first[i, step] = copy
 
     second = []
     for i, (at, w) in enumerate(deep):
         cols = slice(at, at + w)
         value = term[own_rows, cols]
         for step in range(1, n_attn):
-            first[i * (n_attn - 1) + step - 1].wait_recv()
+            first[i, step].wait_recv()
             value += got1[step - 1, :, cols].astype(F32)
         state[:, cols] = value
         rows[0:ROWS, cols] = value.astype(BF16)

time: 27.8 us -> 27.7 us (level)
  no operation moved by 1% of the time
where the time goes in v3:
time: 27.7 us; the launch traced here: 27.5 us
  Pallas kernels  26.8 us (97%)
  local copies, waits for them, and re-layouts  0.66 us (2%)
    pallas_call x1, Pallas kernels, on_device(): pl.pallas_call(functools.partial(layer, n_attn, n_ffn), out_shape=pltpu.V...  26.8 us
    unnamed x1, local copies, waits for them, and re-layouts  0.66 us

profile of v3, /device:TPU:1, one launch (start us, length us, event | category | flops | bytes accessed | tf_op | source)
XLA Modules:
  0.0 27.5 jit_solution(2217780165926290985)
XLA Ops:
  0.0 26.8 %shard_map.91 = bf16[32,2048]{1,0:T(8,128)(2,1)S(1)} custom-call(bf16[128,512]{1,0:T(8,128)(2,1)} %q_hbm.1, bf16[128,512]{1,0:T(8,128)(2,1)} %k_hbm.1, bf16[128,512]{1,0:T(8,128)(2,1)} %v_hbm.1, bf16[128,512]{1,0:T(8,128)(2,1)} %res_hbm.1, s32[1,8]{1,0:T(1,128)} %lens.1, bf16[512,2048]{1,0:T(8,128)(2,1)} %wo_hbm.1, bf16[2048,2048]{1,0:T(8,128)(2,1)} %wg_hbm.1, ...), custom_call_target="tpu_custom_call" | custom-call | flops 1744830464 | bytes 27262976 | tf_op jit(solution)/shard_map/pallas_call | solution.py:341
  26.9 0.7 %copy.11 = bf16[32,2048]{1,0:T(8,128)(2,1)} copy(bf16[32,2048]{1,0:T(8,128)(2,1)S(1)} %shard_map.91) | data formatting | bytes 262144
